TPU v7x, 32 devices: a whole 2x2x4 slice. The times are simulated.
32 devices in a mesh: dp: 4 (over x, core), expert: 8 (over z, y).
Axes of the slice: x: 2, y: 2, z: 4, core: 2. Of those that a mesh axis runs over, the one named last changes fastest.
Arguments:
- tokens: bfloat16 [128, 7168], P(('dp', 'expert')), may hold values from -6 to 6
- routes: int32 [128, 8], P(('dp', 'expert')), may hold values from 0 to 31, all different within a row; in each aligned block of 4 rows (0 to 3, 4 to 7, ...) at most 2 rows name the same one
- gate_scores: float32 [128, 8], P(('dp', 'expert')), may hold values from 0.1 to 1
- w_gate: bfloat16 [32, 7168, 2048], P('expert', None, 'dp'), may hold values from -0.0625 to 0.0625
- w_up: bfloat16 [32, 7168, 2048], P('expert', None, 'dp'), may hold values from -0.0625 to 0.0625
- w_down: bfloat16 [32, 2048, 7168], P('expert', None, 'dp'), may hold values from -0.125 to 0.125
Outputs:
- combined: bfloat16 [128, 7168], P(('dp', 'expert'))
Inputs may be any that keep to these rules, and one draw needn't show every extreme that they name: `routes`: each row names 8 different experts; among the rows of one device no expert is named more than 2 times, a bound that some block reaches.
All inputs are finite; a program needn't handle non-finite values.
Results may differ from a plain program's by a relative error of at most 0.0057.
Values may be sent and summed in bfloat16 or wider, within the bound.
A program may use at most 192 MiB of HBM per device.

v0:
```python
import jax
import jax.numpy as jnp
from jax import lax
from jax.sharding import PartitionSpec as P

D = 7168
TOPK = 8
E = 32
CAP = 2


def slot_codes(route_block):
    route_list = route_block.reshape(-1)
    onehot = (route_list[:, None] == jnp.arange(E, dtype=jnp.int32)[None, :]).astype(jnp.int32)
    before = jnp.cumsum(onehot, axis=0) - onehot
    return (route_list * CAP + jnp.sum(before * onehot, axis=1)).reshape(route_block.shape)


def selection(route_block):
    codes = slot_codes(route_block)
    hits = codes[None, :, :] == jnp.arange(E * CAP, dtype=jnp.int32)[:, None, None]
    return jnp.any(hits, axis=2).astype(jnp.bfloat16)


def expert_hidden(rows_in, gate_local, up_local):
    gate_part = jnp.einsum("erk,ekf->erf", rows_in, gate_local, preferred_element_type=jnp.float32)
    up_part = jnp.einsum("erk,ekf->erf", rows_in, up_local, preferred_element_type=jnp.float32)
    return (jax.nn.silu(gate_part) * up_part).astype(jnp.bfloat16)


def body(tokens, routes, gate_scores, w_gate, w_up, w_down):
    n_data = lax.axis_size("dp")
    n_group = lax.axis_size("expert")
    local_experts = w_gate.shape[0]
    tok_count = tokens.shape[0]
    all_tokens, all_routes = (
        lax.all_gather(tokens, "dp", axis=0, tiled=True),
        lax.all_gather(routes, "dp", axis=0, tiled=True),
    )
    route_blocks = all_routes.reshape(n_data, tok_count, TOPK)
    chosen = jax.vmap(selection)(route_blocks).reshape(n_data, E, CAP, tok_count)
    token_blocks = all_tokens.reshape(n_data, tok_count, D)
    outgoing = jnp.einsum(
        "decn,dnk->edck", chosen, token_blocks, preferred_element_type=jnp.float32
    ).astype(jnp.bfloat16)
    arrived = lax.all_to_all(outgoing, "expert", split_axis=0, concat_axis=2, tiled=True)
    items = arrived.shape[1]
    merged = arrived.reshape(local_experts, items * arrived.shape[2], D)
    result = expert_hidden(merged, w_gate, w_up)
    hidden_split = result.reshape(local_experts, items, arrived.shape[2], w_gate.shape[2])
    hidden = hidden_split.reshape(local_experts, n_data * n_group * CAP, w_gate.shape[2])
    width_local = w_down.shape[2]
    expert_out = jnp.einsum(
        "erf,efk->erk",
        lax.all_gather(hidden, "dp", axis=2, tiled=True),
        w_down,
        preferred_element_type=jnp.float32,
    ).astype(jnp.bfloat16)
    expert_out = expert_out.reshape(local_experts, n_data, n_group, CAP, width_local)
    returned = lax.all_to_all(
        lax.all_to_all(expert_out, "dp", split_axis=1, concat_axis=4, tiled=True),
        "expert",
        split_axis=2,
        concat_axis=0,
        tiled=True,
    )
    returned = returned.reshape(E * CAP, D)
    codes = slot_codes(routes)
    matches = codes[:, :, None] == jnp.arange(E * CAP, dtype=jnp.int32)[None, None, :]
    weighting = jnp.sum(jnp.where(matches, gate_scores[:, :, None], 0.0), axis=1)
    combined = jnp.dot(weighting, returned.astype(jnp.float32), precision=lax.Precision.HIGHEST)
    return combined.astype(jnp.bfloat16)


def solution(mesh):
    placed = (
        P(("dp", "expert"), None),
        P(("dp", "expert"), None),
        P(("dp", "expert"), None),
        P("expert", None, "dp"),
        P("expert", None, "dp"),
        P("expert", None, "dp"),
    )
    return jax.shard_map(
        body, mesh=mesh, in_specs=placed, out_specs=P(("dp", "expert"), None), check_vma=False
    )
```

profile of v0, /device:TPU:0, one launch (start us, length us, event | category | flops | bytes accessed | tf_op | source)
XLA Modules:
  0.0 237.9 jit_solution(15998013190049495341)
XLA Ops:
  6.5 0.0 all-gather.4.cloned.1.call-start
  6.5 6.3 %all-gather = s32[4,4,8]{2,1,0:T(4,128)S(1)} all-gather(s32[1,4,8]{2,1,0:T(4,128)} %bitcast.38), channel_id=1, replica_groups=mesh['dp'=4,'expert'=8] {'dp'}, dimensions={0}, use_global_device_ids=true | all-gather | bytes 640 | tf_op jit(solution)/shard_map/all_gather | solution.py:38
  12.8 0.1 eq.63
  12.9 0.1 fusion.4
  13.0 0.1 reduce_window_sum.23
  13.0 0.2 select_reduce_fusion
  13.3 0.1 reduce_sum.35
  13.4 0.1 fusion.5
  13.5 0.1 copy.18
  13.6 6.3 %all-gather.1 = bf16[4,4,7168]{2,1,0:T(4,128)(2,1)S(1)} all-gather(bf16[1,4,7168]{2,1,0:T(4,128)(2,1)} %bitcast.37), channel_id=1, replica_groups=mesh['dp'=4,'expert'=8] {'dp'}, dimensions={0}, use_global_device_ids=true | all-gather | bytes 286720 | tf_op jit(solution)/shard_map/all_gather | solution.py:37
  19.9 1.1 fusion
  21.0 3.8 %copy.20 = bf16[32,4,2,7168]{3,2,1,0:T(2,128)(2,1)S(1)} copy(bf16[32,4,2,7168]{3,0,2,1:T(8,128)(2,1)S(1)} %fusion) | data formatting | bytes 7340032 | tf_op jit(solution)/shard_map/convert_element_type | solution.py:45
  24.8 88.2 %all_to_all.48 = bf16[32,4,2,7168]{3,2,1,0:T(2,128)(2,1)S(1)} all-to-all(bf16[32,4,2,7168]{3,2,1,0:T(2,128)(2,1)S(1)} %copy.20), channel_id=1, replica_groups=mesh['dp'=4,'expert'=8] {'expert'}, dimensions={0} | all-to-all | bytes 7340032 | tf_op jit(solution)/shard_map/all_to_all | solution.py:46
  112.9 5.5 %copy.31 = bf16[8,4,4,2,7168]{4,3,0,2,1:T(2,128)(2,1)} copy(bf16[8,4,4,2,7168]{4,3,2,1,0:T(2,128)(2,1)S(1)} %bitcast.32) | data formatting | bytes 7340032 | tf_op jit(solution)/shard_map/all_to_all | solution.py:46
  118.4 8.4 %reshape.42 = bf16[4,64,7168]{2,1,0:T(8,128)(2,1)} reshape(bf16[4,4,8,2,7168]{4,3,2,1,0:T(2,128)(2,1)} %bitcast.33) | data formatting | bytes 7340032 | tf_op jit(solution)/shard_map/reshape | solution.py:48
  126.8 0.0 copy-start
  126.8 13.1 %fusion.7 = f32[4,64,512]{2,1,0:T(8,128)S(1)} fusion(bf16[4,64,7168]{2,1,0:T(8,128)(2,1)} %reshape.42, bf16[4,7168,512]{2,1,0:T(8,128)(2,1)} %param.9), kind=kOutput, calls=%fused_computation.21 | convolution fusion | flops 1879048192 | bytes 33554432 | tf_op jit(solution)/shard_map/erk,ekf->erf/dot_general | solution.py:26
  139.9 0.0 copy-done
  139.9 12.9 %fusion.1 = bf16[4,64,512]{2,1,0:T(8,128)(2,1)} fusion(bf16[4,64,7168]{2,1,0:T(8,128)(2,1)S(1)} %copy-done, bf16[4,7168,512]{2,1,0:T(8,128)(2,1)} %param.10, f32[4,64,512]{2,1,0:T(8,128)S(1)} %fusion.7), kind=kOutput, calls=%fused_computation.6 | convolution fusion | flops 1879834624 | bytes 33816576 | tf_op jit(solution)/shard_map/erk,ekf->erf/dot_general | solution.py:27
  152.8 0.0 all-gather.4.cloned.1.call-update
  152.8 15.9 %all-gather.4.cloned.1.call-done = bf16[4,64,2048]{2,1,0:T(8,128)(2,1)} async-done(((bf16[4,64,512]{2,1,0:T(8,128)(2,1)}), bf16[4,64,2048]{2,1,0:T(8,128)(2,1)}) %all-gather.4.cloned.1.call-update) | async-done | bytes 1048592 | tf_op jit(solution)/shard_map/all_gather | solution.py:55
  168.8 14.6 %convolution_convert_fusion.2 = bf16[4,64,1792]{2,1,0:T(8,128)(2,1)S(1)} fusion(bf16[4,64,2048]{2,1,0:T(8,128)(2,1)} %all-gather.4.cloned.1.call-done, bf16[4,2048,1792]{2,1,0:T(8,128)(2,1)} %param.11), kind=kOutput, calls=%fused_computation.4 | convolution fusion | flops 1879506944 | bytes 31326208 | tf_op jit(solution)/shard_map/erf,efk->erk/dot_general | solution.py:53
  183.4 0.0 copy-start.1
  183.4 0.0 copy-start.2
  183.4 0.3 reshape.43
  183.8 0.1 copy.22
  183.9 15.5 %all_to_all.49 = bf16[4,4,8,2,1792]{4,2,3,0,1:T(8,128)(2,1)S(1)} all-to-all(bf16[4,4,8,2,1792]{4,2,3,0,1:T(8,128)(2,1)S(1)} %copy.22), channel_id=1, replica_groups=mesh['dp'=4,'expert'=8] {'dp'}, dimensions={1} | all-to-all | bytes 1835008 | tf_op jit(solution)/shard_map/all_to_all | solution.py:61
  199.3 0.7 copy.26
  200.1 1.3 reshape.55
  201.3 5.5 %all-to-all-start.2 = ((bf16[4,1,8,2,7168]{4,3,0,1,2:T(2,128)(2,1)}), bf16[4,1,8,2,7168]{4,3,0,1,2:T(2,128)(2,1)S(1)}, u32[]{:S(2)}, u32[]{:S(2)}) async-start(bf16[4,1,8,2,7168]{4,3,0,1,2:T(2,128)(2,1)} %reshape.55), calls=%async_computation.2 | async-start | bytes 1835008 | tf_op jit(solution)/shard_map/all_to_all | solution.py:60
  206.8 0.0 copy-done.1
  206.8 0.1 eq.56
  206.9 0.1 fusion.6
  207.0 0.1 reduce_window_sum.22
  207.1 0.2 select_reduce_fusion.2
  207.2 0.1 reduce_sum.32
  207.3 0.0 copy-done.2
  207.3 0.1 select_reduce_fusion.1
  207.4 22.2 %all-to-all-done.2 = bf16[4,1,8,2,7168]{4,3,0,1,2:T(2,128)(2,1)S(1)} async-done(((bf16[4,1,8,2,7168]{4,3,0,1,2:T(2,128)(2,1)}), bf16[4,1,8,2,7168]{4,3,0,1,2:T(2,128)(2,1)S(1)}, u32[]{:S(2)}, u32[]{:S(2)}) %all-to-all-start.2) | async-done | bytes 917536 | tf_op jit(solution)/shard_map/all_to_all | solution.py:60
  229.7 0.3 reshape.44
  230.0 1.1 convolution_convert_fusion.1
  (2 shorter events, 0.0 us)
Async XLA Ops:
  6.5 162.2 %all-gather.4.cloned.1.call-start = ((), (), s32[]{:S(2)}) async-start(), calls=%async_computation.3 | async-start | bytes 1310720 | tf_op jit(solution)/shard_map/all_gather | solution.py:55
  126.8 13.1 %copy-start = (bf16[4,64,7168]{2,1,0:T(8,128)(2,1)S(1)}, bf16[4,64,7168]{2,1,0:T(8,128)(2,1)}, u32[]{:S(2)}) copy-start(bf16[4,64,7168]{2,1,0:T(8,128)(2,1)} %reshape.42) | copy-start | bytes 11010052
  183.4 23.5 %copy-start.1 = (s32[4,8]{1,0:T(4,128)S(1)}, s32[4,8]{1,0:T(4,128)}, u32[]{:S(2)}) copy-start(s32[4,8]{1,0:T(4,128)} %param.7) | copy-start | bytes 388
  183.4 23.9 %copy-start.2 = (f32[4,8]{1,0:T(4,128)S(1)}, f32[4,8]{1,0:T(4,128)}, u32[]{:S(2)}) copy-start(f32[4,8]{1,0:T(4,128)} %param.8) | copy-start | bytes 388
  201.3 28.3 %all-to-all-start.2 = ((bf16[4,1,8,2,7168]{4,3,0,1,2:T(2,128)(2,1)}), bf16[4,1,8,2,7168]{4,3,0,1,2:T(2,128)(2,1)S(1)}, u32[]{:S(2)}, u32[]{:S(2)}) async-start(bf16[4,1,8,2,7168]{4,3,0,1,2:T(2,128)(2,1)} %reshape.55), calls=%async_computation.2 | async-start | bytes 1835008 | tf_op jit(solution)/shard_map/all_to_all | solution.py:60
Sparse Core Ops, SparseCore 0:
  152.9 15.7 all-gather.3
where the time goes:
time: 238 us
  blocking collectives  116 us (49%)
  matrix products  42.8 us (18%)
  waiting for transfers between devices  38.2 us (16%)
  local copies, waits for them, and re-layouts  20.9 us (9%)
  between operations  13.5 us (6%)
  starting transfers between devices  5.52 us (2%)
    all_to_all x1, blocking collectives, body(): lax.all_to_all(outgoing, 'expert', split_axis=0, concat_axis=2, tiled=True)  88.2 us
    all_to_all x1, waiting for transfers between devices, body(): lax.all_to_all(lax.all_to_all(expert_out, 'dp', split_axis=1, concat_axis...  22.2 us
    all_gather x1, waiting for transfers between devices, body(): lax.all_gather(hidden, 'dp', axis=2, tiled=True)  15.9 us
    all_to_all x1, blocking collectives, body(): lax.all_to_all(expert_out, 'dp', split_axis=1, concat_axis=4, tiled=True)  15.5 us
    dot_general x1, matrix products, body(): jnp.einsum('erf,efk->erk', lax.all_gather(hidden, 'dp', axis=2, tiled=Tru...  14.6 us
    dot_general x1, matrix products, expert_hidden(): jnp.einsum('erk,ekf->erf', rows_in, gate_local, preferred_element_type=jn...  13.1 us
    dot_general x1, matrix products, expert_hidden(): jnp.einsum('erk,ekf->erf', rows_in, up_local, preferred_element_type=jnp....  12.9 us
    reshape x1, local copies, waits for them, and re-layouts, body(): merged = arrived.reshape(local_experts, items * arrived.shape[2], D)  8.4 us
  transfers between devices with their start and end apart: 2, of which 2 were waited for; matrix products, arithmetic and copies ran while one was open for 0% of the time, Pallas kernels for 0%

commit v1 on v0

--- a/solution.py
+++ b/solution.py
@@ -7,6 +7,22 @@
 TOPK = 8
 E = 32
 CAP = 2
+
+
+def ring_product(x, axis, dim, term):
+    size, index, span = (lax.axis_size(axis), lax.axis_index(axis), x.shape[dim])
+    right = [(i, (i + 1) % size) for i in range(size)]
+    downward = [(i, (i - 1) % size) for i in range(size)]
+    half = size // 2
+    from_left = from_right = x
+    running = term(x, index * span)
+    for step in range(1, half + 1):
+        from_left = lax.ppermute(from_left, axis, right)
+        if step < size - half:
+            from_right = lax.ppermute(from_right, axis, downward)
+            running = running + term(from_right, (index + step) % size * span)
+        running = running + term(from_left, (index - step) % size * span)
+    return running
 
 
 def slot_codes(route_block):
@@ -50,11 +66,16 @@
     hidden_split = result.reshape(local_experts, items, arrived.shape[2], w_gate.shape[2])
     hidden = hidden_split.reshape(local_experts, n_data * n_group * CAP, w_gate.shape[2])
     width_local = w_down.shape[2]
-    expert_out = jnp.einsum(
-        "erf,efk->erk",
-        lax.all_gather(hidden, "dp", axis=2, tiled=True),
-        w_down,
-        preferred_element_type=jnp.float32,
+    expert_out = ring_product(
+        hidden,
+        "dp",
+        2,
+        lambda shard, start: jnp.einsum(
+            "erf,efk->erk",
+            shard,
+            lax.dynamic_slice_in_dim(w_down, start, shard.shape[2], axis=1),
+            preferred_element_type=jnp.float32,
+        ),
     ).astype(jnp.bfloat16)
     expert_out = expert_out.reshape(local_experts, n_data, n_group, CAP, width_local)
     returned = lax.all_to_all(

time: 238 us -> 218 us (0.916)
  blocking collectives: 116 us -> 29.1 us
  waiting for transfers between devices: 38.2 us -> 105 us
  between operations: 13.5 us -> 0.14 us
  starting transfers between devices: 5.52 us -> 11.6 us
  local copies, waits for them, and re-layouts: 20.9 us -> 24.7 us
  matrix products: 42.8 us -> 45.4 us
    all_to_all x1 -> x0, blocking collectives: 88.2 us -> none  [body(): lax.all_to_all(outgoing, 'expert', split_axis=0, concat_axis=2, tiled=True)]
    all_to_all x0 -> x1, waiting for transfers between devices: none -> 82.6 us  [body(): lax.all_to_all(outgoing, 'expert', split_axis=0, concat_axis=2, tiled=True)]
    all_gather x1 -> x0, waiting for transfers between devices: 15.9 us -> none  [body(): lax.all_gather(hidden, 'dp', axis=2, tiled=True)]
    all_to_all x0 -> x1, starting transfers between devices: none -> 5.96 us  [body(): lax.all_to_all(outgoing, 'expert', split_axis=0, concat_axis=2, tiled=True)]
    dot_general x1 -> x4, matrix products: 14.6 us -> 17.9 us  [body(): jnp.einsum('erf,efk->erk', shard, lax.dynamic_slice_in_dim(w_down, start,...]
  transfers between devices with their start and end apart: 2 -> 5, of which waited for: 2 -> 3; matrix products, arithmetic and copies ran while one was open for 0% -> 6% of each run, Pallas kernels for 0% -> 0%
where the time goes in v1:
time: 218 us; the launch traced here: 217 us
  waiting for transfers between devices  105 us (48%)
  matrix products  45.4 us (21%)
  blocking collectives  29.1 us (13%)
  local copies, waits for them, and re-layouts  24.7 us (11%)
  starting transfers between devices  11.6 us (5%)
    all_to_all x1, waiting for transfers between devices, body(): lax.all_to_all(outgoing, 'expert', split_axis=0, concat_axis=2, tiled=True)  82.6 us
    all_to_all x1, waiting for transfers between devices, body(): lax.all_to_all(lax.all_to_all(expert_out, 'dp', split_axis=1, concat_axis...  22.3 us
    dot_general x4, matrix products, body(): jnp.einsum('erf,efk->erk', shard, lax.dynamic_slice_in_dim(w_down, start,...  17.9 us
    all_to_all x1, blocking collectives, body(): lax.all_to_all(expert_out, 'dp', split_axis=1, concat_axis=4, tiled=True)  16.6 us
    dot_general x1, matrix products, expert_hidden(): jnp.einsum('erk,ekf->erf', rows_in, gate_local, preferred_element_type=jn...  13.1 us
    dot_general x1, matrix products, expert_hidden(): jnp.einsum('erk,ekf->erf', rows_in, up_local, preferred_element_type=jnp....  12.2 us
    reshape x1, local copies, waits for them, and re-layouts, body(): merged = arrived.reshape(local_experts, items * arrived.shape[2], D)  8.4 us
    all_to_all x1, local copies, waits for them, and re-layouts, body(): lax.all_to_all(outgoing, 'expert', split_axis=0, concat_axis=2, tiled=True)  7.41 us
  transfers between devices with their start and end apart: 5, of which 3 were waited for; matrix products, arithmetic and copies ran while one was open for 6% of the time, Pallas kernels for 0%

profile of v1, /device:TPU:0, one launch (start us, length us, event | category | flops | bytes accessed | tf_op | source)
XLA Modules:
  0.0 217.2 jit_solution(7696155670127710246)
XLA Ops:
  0.0 6.3 %all-gather = s32[4,4,8]{2,1,0:T(4,128)S(1)} all-gather(s32[1,4,8]{2,1,0:T(4,128)} %bitcast.39), channel_id=1, replica_groups=mesh['dp'=4,'expert'=8] {'dp'}, dimensions={0}, use_global_device_ids=true | all-gather | bytes 640 | tf_op jit(solution)/shard_map/all_gather | solution.py:54
  6.3 0.1 eq.67
  6.3 0.1 fusion.24
  6.4 0.1 reduce_window_sum.23
  6.5 0.2 select_reduce_fusion
  6.7 0.1 reduce_sum.35
  6.8 0.1 fusion.25
  6.9 0.1 copy.18
  7.1 6.3 %all-gather.1 = bf16[4,4,7168]{2,1,0:T(4,128)(2,1)S(1)} all-gather(bf16[1,4,7168]{2,1,0:T(4,128)(2,1)} %bitcast.38), channel_id=1, replica_groups=mesh['dp'=4,'expert'=8] {'dp'}, dimensions={0}, use_global_device_ids=true | all-gather | bytes 286720 | tf_op jit(solution)/shard_map/all_gather | solution.py:53
  13.4 1.1 fusion
  14.4 5.6 %copy.20 = bf16[32,4,2,7168]{3,2,1,0:T(2,128)(2,1)} copy(bf16[32,4,2,7168]{3,0,2,1:T(8,128)(2,1)S(1)} %fusion) | data formatting | bytes 7340032 | tf_op jit(solution)/shard_map/convert_element_type | solution.py:61
  20.0 6.0 %all-to-all-start = ((bf16[32,4,2,7168]{3,2,1,0:T(2,128)(2,1)}), bf16[32,4,2,7168]{3,2,1,0:T(2,128)(2,1)}, u32[]{:S(2)}, u32[]{:S(2)}) async-start(bf16[32,4,2,7168]{3,2,1,0:T(2,128)(2,1)} %copy.20), calls=%async_computation | async-start | bytes 7340032 | tf_op jit(solution)/shard_map/all_to_all | solution.py:62
  26.0 82.6 %all-to-all-done = bf16[32,4,2,7168]{3,2,1,0:T(2,128)(2,1)} async-done(((bf16[32,4,2,7168]{3,2,1,0:T(2,128)(2,1)}), bf16[32,4,2,7168]{3,2,1,0:T(2,128)(2,1)}, u32[]{:S(2)}, u32[]{:S(2)}) %all-to-all-start) | async-done | bytes 3670048 | tf_op jit(solution)/shard_map/all_to_all | solution.py:62
  108.6 7.4 %copy.31 = bf16[8,4,4,2,7168]{4,3,0,2,1:T(2,128)(2,1)} copy(bf16[8,4,4,2,7168]{4,3,2,1,0:T(2,128)(2,1)} %bitcast.6) | data formatting | bytes 7340032 | tf_op jit(solution)/shard_map/all_to_all | solution.py:62
  116.0 8.4 %reshape.42 = bf16[4,64,7168]{2,1,0:T(8,128)(2,1)} reshape(bf16[4,4,8,2,7168]{4,3,2,1,0:T(2,128)(2,1)} %bitcast.34) | data formatting | bytes 7340032 | tf_op jit(solution)/shard_map/reshape | solution.py:64
  124.4 0.0 copy-start
  124.4 13.1 %fusion.31 = f32[4,64,512]{2,1,0:T(8,128)S(1)} fusion(bf16[4,64,7168]{2,1,0:T(8,128)(2,1)} %reshape.42, bf16[4,7168,512]{2,1,0:T(8,128)(2,1)} %param.9), kind=kOutput, calls=%fused_computation.36 | convolution fusion | flops 1879048192 | bytes 33554432 | tf_op jit(solution)/shard_map/erk,ekf->erf/dot_general | solution.py:42
  137.5 0.0 copy-done
  137.5 12.2 %fusion.21 = bf16[4,64,512]{2,1,0:T(8,128)(2,1)S(1)} fusion(bf16[4,64,7168]{2,1,0:T(8,128)(2,1)S(1)} %copy-done, bf16[4,7168,512]{2,1,0:T(8,128)(2,1)} %param.10, f32[4,64,512]{2,1,0:T(8,128)S(1)} %fusion.31), kind=kOutput, calls=%fused_computation.17 | convolution fusion | flops 1879834624 | bytes 33816576 | tf_op jit(solution)/shard_map/erk,ekf->erf/dot_general | solution.py:43
  149.7 0.1 collective-permute-start.1
  149.7 1.7 collective-permute-start
  151.5 4.5 %fusion.7 = f32[4,64,1792]{2,1,0:T(8,128)S(1)} fusion(bf16[4,64,512]{2,1,0:T(8,128)(2,1)S(1)} %fusion.21, bf16[4,2048,1792]{2,1,0:T(8,128)(2,1)} %param.11, s32[]{:T(128)S(6)} %select_n.32), kind=kOutput, calls=%fused_computation.9 | convolution fusion | flops 469762048 | bytes 9437188 | tf_op jit(solution)/shard_map/erf,efk->erk/dot_general | solution.py:73
  155.9 0.5 collective-permute-done.1
  156.5 0.2 collective-permute-start.2
  156.7 4.5 %fusion.3 = f32[4,64,1792]{2,1,0:T(8,128)S(1)} fusion(bf16[4,64,512]{2,1,0:T(8,128)(2,1)S(1)} %collective-permute-done.1, bf16[4,2048,1792]{2,1,0:T(8,128)(2,1)} %param.11, s32[]{:T(128)S(6)} %select_n.36), kind=kOutput, calls=%fused_computation.5 | convolution fusion | flops 469762048 | bytes 9437188 | tf_op jit(solution)/shard_map/erf,efk->erk/dot_general | solution.py:73
  161.1 0.0 collective-permute-done
  161.1 4.5 %fusion.12 = f32[4,64,1792]{2,1,0:T(8,128)S(1)} fusion(f32[4,64,1792]{2,1,0:T(8,128)S(1)} %fusion.3, f32[4,64,1792]{2,1,0:T(8,128)S(1)} %fusion.7, bf16[4,64,512]{2,1,0:T(8,128)(2,1)S(1)} %collective-permute-done, bf16[4,2048,1792]{2,1,0:T(8,128)(2,1)} %param.11, s32[]{:T(128)S(6)} %select_n.34), kind=kOutput, calls=%fused_computation.13 | convolution fusion | flops 470679552 | bytes 13107204 | tf_op jit(solution)/shard_map/erf,efk->erk/dot_general | solution.py:73
  165.7 0.0 collective-permute-done.2
  165.7 4.5 %fusion.18 = bf16[4,64,1792]{2,1,0:T(8,128)(2,1)S(1)} fusion(f32[4,64,1792]{2,1,0:T(8,128)S(1)} %fusion.12, bf16[4,64,512]{2,1,0:T(8,128)(2,1)S(1)} %collective-permute-done.2, bf16[4,2048,1792]{2,1,0:T(8,128)(2,1)} %param.11, s32[]{:T(128)S(6)} %select_n.38), kind=kOutput, calls=%fused_computation.15 | convolution fusion | flops 470679552 | bytes 10354692 | tf_op jit(solution)/shard_map/erf,efk->erk/dot_general | solution.py:73
  170.1 0.0 copy-start.1
  170.2 0.0 copy-start.2
  170.2 0.3 reshape.43
  170.5 0.1 copy.22
  170.6 16.6 %all_to_all.48 = bf16[4,4,8,2,1792]{4,2,3,0,1:T(8,128)(2,1)S(1)} all-to-all(bf16[4,4,8,2,1792]{4,2,3,0,1:T(8,128)(2,1)S(1)} %copy.22), channel_id=1, replica_groups=mesh['dp'=4,'expert'=8] {'dp'}, dimensions={1} | all-to-all | bytes 1835008 | tf_op jit(solution)/shard_map/all_to_all | solution.py:82
  187.2 0.7 copy.26
  187.9 1.3 reshape.55
  189.2 3.6 %all-to-all-start.2 = ((bf16[4,1,8,2,7168]{4,3,0,1,2:T(2,128)(2,1)}), bf16[4,1,8,2,7168]{4,3,0,1,2:T(2,128)(2,1)S(1)}, u32[]{:S(2)}, u32[]{:S(2)}) async-start(bf16[4,1,8,2,7168]{4,3,0,1,2:T(2,128)(2,1)} %reshape.55), calls=%async_computation.2 | async-start | bytes 1835008 | tf_op jit(solution)/shard_map/all_to_all | solution.py:81
  192.8 0.0 copy-done.1
  192.9 0.1 eq.60
  192.9 0.1 fusion.26
  193.0 0.1 reduce_window_sum.22
  193.1 0.2 select_reduce_fusion.2
  193.2 0.1 reduce_sum.32
  193.3 0.0 copy-done.2
  193.3 0.1 select_reduce_fusion.1
  193.4 22.3 %all-to-all-done.2 = bf16[4,1,8,2,7168]{4,3,0,1,2:T(2,128)(2,1)S(1)} async-done(((bf16[4,1,8,2,7168]{4,3,0,1,2:T(2,128)(2,1)}), bf16[4,1,8,2,7168]{4,3,0,1,2:T(2,128)(2,1)S(1)}, u32[]{:S(2)}, u32[]{:S(2)}) %all-to-all-start.2) | async-done | bytes 917536 | tf_op jit(solution)/shard_map/all_to_all | solution.py:81
  215.7 0.3 reshape.44
  216.1 1.1 convolution_convert_fusion.1
  (2 shorter events, 0.0 us)
Async XLA Ops:
  20.0 88.5 %all-to-all-start = ((bf16[32,4,2,7168]{3,2,1,0:T(2,128)(2,1)}), bf16[32,4,2,7168]{3,2,1,0:T(2,128)(2,1)}, u32[]{:S(2)}, u32[]{:S(2)}) async-start(bf16[32,4,2,7168]{3,2,1,0:T(2,128)(2,1)} %copy.20), calls=%async_computation | async-start | bytes 7340032 | tf_op jit(solution)/shard_map/all_to_all | solution.py:62
  124.4 13.1 %copy-start = (bf16[4,64,7168]{2,1,0:T(8,128)(2,1)S(1)}, bf16[4,64,7168]{2,1,0:T(8,128)(2,1)}, u32[]{:S(2)}) copy-start(bf16[4,64,7168]{2,1,0:T(8,128)(2,1)} %reshape.42) | copy-start | bytes 11010052
  149.7 6.8 %collective-permute-start.1 = (bf16[4,64,512]{2,1,0:T(8,128)(2,1)S(1)}, bf16[4,64,512]{2,1,0:T(8,128)(2,1)S(1)}, u32[]{:S(2)}, u32[]{:S(2)}) collective-permute-start(bf16[4,64,512]{2,1,0:T(8,128)(2,1)S(1)} %fusion.21), channel_id=1, source_target_pairs={{0,8},{8,16},{16,24},{24,0},{1,9},{9,17},{17,25},{25,1},{2,10},{10... | collective-permute-start | bytes 786440 | tf_op jit(solution)/shard_map/ppermute | solution.py:20
  149.7 11.4 %collective-permute-start = (bf16[4,64,512]{2,1,0:T(8,128)(2,1)S(1)}, bf16[4,64,512]{2,1,0:T(8,128)(2,1)S(1)}, u32[]{:S(2)}, u32[]{:S(2)}) collective-permute-start(bf16[4,64,512]{2,1,0:T(8,128)(2,1)S(1)} %fusion.21), channel_id=1, source_target_pairs={{0,24},{8,0},{16,8},{24,16},{1,25},{9,1},{17,9},{25,17},{2,26},{10... | collective-permute-start | bytes 786440 | tf_op jit(solution)/shard_map/ppermute | solution.py:22
  156.5 9.2 %collective-permute-start.2 = (bf16[4,64,512]{2,1,0:T(8,128)(2,1)S(1)}, bf16[4,64,512]{2,1,0:T(8,128)(2,1)S(1)}, u32[]{:S(2)}, u32[]{:S(2)}) collective-permute-start(bf16[4,64,512]{2,1,0:T(8,128)(2,1)S(1)} %collective-permute-done.1), channel_id=1, source_target_pairs={{0,8},{8,16},{16,24},{24,0},{1,9},{9,17},{17,25},{25,1},{2,10},{10... | collective-permute-start | bytes 786440 | tf_op jit(solution)/shard_map/ppermute | solution.py:20
  170.1 22.7 %copy-start.1 = (s32[4,8]{1,0:T(4,128)S(1)}, s32[4,8]{1,0:T(4,128)}, u32[]{:S(2)}) copy-start(s32[4,8]{1,0:T(4,128)} %param.7) | copy-start | bytes 388
  170.2 23.2 %copy-start.2 = (f32[4,8]{1,0:T(4,128)S(1)}, f32[4,8]{1,0:T(4,128)}, u32[]{:S(2)}) copy-start(f32[4,8]{1,0:T(4,128)} %param.8) | copy-start | bytes 388
  189.2 26.5 %all-to-all-start.2 = ((bf16[4,1,8,2,7168]{4,3,0,1,2:T(2,128)(2,1)}), bf16[4,1,8,2,7168]{4,3,0,1,2:T(2,128)(2,1)S(1)}, u32[]{:S(2)}, u32[]{:S(2)}) async-start(bf16[4,1,8,2,7168]{4,3,0,1,2:T(2,128)(2,1)} %reshape.55), calls=%async_computation.2 | async-start | bytes 1835008 | tf_op jit(solution)/shard_map/all_to_all | solution.py:81
